TPU v7x, 256 devices: a whole 4x4x8 slice. The times are simulated.
256 devices in a mesh: replica: 16 (over x_lo, y, core), tensor: 16 (over x_hi, z).
Axes of the slice: x: 4 (x_hi: 2, x_lo: 2; x = x_hi * 2 + x_lo), y: 4, z: 8, core: 2. Of those that a mesh axis runs over, the one named last changes fastest.
Arguments:
- params: bfloat16 [16, 4096, 4096], P('replica', None, 'tensor'), may hold values from -6 to 6
- anchor: float32 [512, 4096], P(None, 'tensor'), may hold values from -6 to 6
- momentum: float32 [512, 4096], P(None, 'tensor'), may hold values from -4 to 4
- tokens: bfloat16 [16, 1, 2048, 4096], P('replica', None, 'tensor'), may hold values from -6 to 6
- fragment: int32 [1], replicated, may hold values from 0 to 7
Outputs:
- params_out: bfloat16 [16, 4096, 4096], P('replica', None, 'tensor')
- momentum_out: float32 [512, 4096], P(None, 'tensor')
- anchor_out: float32 [512, 4096], P(None, 'tensor')
Inputs may be any that keep to these rules, and one draw needn't show every extreme that they name: `fragment`: the index of one of the 8 fragments.
All inputs are finite; a program needn't handle non-finite values.
Results may differ from a plain program's by a relative error of at most 0.0034.
Values may be sent and summed in bfloat16 or wider, within the bound.
A program may use at most 64 MiB of HBM per device.

v0:
```python
import math

import jax
import jax.numpy as jnp
from jax import lax
from jax.sharding import PartitionSpec as P

FRAGMENTS = 8


inner_rate = 128.0
outer_rate = 0.7
nesterov_mu = 0.9


def fold_rows(weight, col_first, shard_rows):
    inv_root = 1.0 / math.sqrt(weight.shape[0])
    outputs = jnp.dot(shard_rows, weight, preferred_element_type=jnp.float32) * inv_root
    target = lax.dynamic_slice_in_dim(shard_rows, col_first, weight.shape[1], 1).astype(jnp.float32)
    residual = (outputs - target).astype(jnp.bfloat16)
    return lax.dot_general(
        shard_rows, residual, (((0,), (0,)), ((), ())), preferred_element_type=jnp.float32
    )


def apply_step(weight, gradient, total_rows):
    inv_root = 1.0 / math.sqrt(weight.shape[0])
    scaled = gradient * (inv_root / total_rows)
    return (weight.astype(jnp.float32) - inner_rate * scaled).astype(jnp.bfloat16)


def local(params, anchor, momentum, tokens, fragment):
    weight = params[0]
    batches = tokens[0]
    width = weight.shape[0]
    columns = weight.shape[1]
    col_first = lax.axis_index("tensor") * columns
    total_rows = batches.shape[1] * lax.axis_size("tensor")
    frag_rows = width // FRAGMENTS
    first_row = fragment[0] * frag_rows
    before = weight
    before_rows = lax.dynamic_slice_in_dim(before, first_row, frag_rows, 0).astype(jnp.float32)
    drift = anchor - before_rows
    summed = lax.psum(drift, "replica")
    outer_grad = summed / lax.axis_size("replica")
    momentum_out = nesterov_mu * momentum + outer_grad
    anchor_out = anchor - outer_rate * (outer_grad + nesterov_mu * momentum_out)
    gradient = fold_rows(
        weight, col_first, lax.all_gather(batches[0], "tensor", axis=0, tiled=True)
    )
    weight = apply_step(weight, gradient, total_rows)
    before_rows = lax.dynamic_slice_in_dim(before, first_row, frag_rows, 0).astype(jnp.float32)
    after_rows = lax.dynamic_slice_in_dim(weight, first_row, frag_rows, 0).astype(jnp.float32)
    merged = (anchor_out + (after_rows - before_rows)).astype(jnp.bfloat16)
    params_out = lax.dynamic_update_slice_in_dim(weight, merged, first_row, 0)
    return (params_out[None], momentum_out, anchor_out)


def solution(mesh):
    return jax.shard_map(
        local,
        mesh=mesh,
        in_specs=(
            P("replica", None, "tensor"),
            P(None, "tensor"),
            P(None, "tensor"),
            P("replica", None, "tensor", None),
            P(),
        ),
        out_specs=(P("replica", None, "tensor"), P(None, "tensor"), P(None, "tensor")),
        check_vma=False,
    )
```

profile of v0, /device:TPU:1, one launch (start us, length us, event | category | flops | bytes accessed | tf_op | source)
XLA Modules:
  0.0 288.3 jit_solution(10236285234908716945)
XLA Ops:
  8.0 0.0 copy-start.3
  8.0 0.0 all-reduce.2.cloned.1.call-start
  8.1 3.0 %copy.8 = bf16[1,4096,256]{1,2,0:T(8,128)(2,1)S(1)} copy(bf16[1,4096,256]{2,1,0:T(8,128)(2,1)} %param.5) | data formatting | bytes 4194304 | tf_op args[0]
  11.0 0.0 copy-start
  11.7 0.0 copy-done.3
  11.7 0.2 copy.12
  11.9 0.9 convert_subtract_fusion.1
  12.8 0.0 all-reduce.2.cloned.1.call-update
  12.8 0.0 all-gather.3.cloned.1.call-start
  12.9 0.5 all-gather.3.cloned.1.call-update
  13.4 1.2 copy.11
  14.6 213.9 %all-reduce.2.cloned.1.call-done = f32[512,256]{0,1:T(8,128)} async-done(((f32[512,256]{0,1:T(8,128)}), f32[512,256]{0,1:T(8,128)}) %all-reduce.2.cloned.1.call-update) | async-done | bytes 524304 | tf_op jit(solution)/shard_map/psum | solution.py:44
  228.5 1.9 multiply_add_fusion
  230.5 2.0 copy.14
  232.5 11.3 %all-gather.3.cloned.1.call-done = bf16[1,1,2048,4096]{3,2,1,0:T(8,128)(2,1)} async-done(((bf16[1,1,128,4096]{3,2,1,0:T(8,128)(2,1)}), bf16[1,1,2048,4096]{3,2,1,0:T(8,128)(2,1)}) %all-gather.3.cloned.1.call-update) | async-done | bytes 16777232 | tf_op jit(solution)/shard_map/all_gather | solution.py:49
  243.8 0.0 copy-done
  243.8 29.9 %fusion.13 = bf16[4096,256]{0,1:T(8,128)(2,1)} fusion(bf16[1,1,2048,4096]{3,2,1,0:T(8,128)(2,1)} %all-gather.3.cloned.1.call-done, bf16[1,4096,256]{2,1,0:T(8,128)(2,1)} %param.5, bf16[1,4096,256]{1,2,0:T(8,128)(2,1)S(1)} %copy.8, s32[]{:T(128)S(6)} %select_n.4), kind=kOutput, calls=%fused_computation.7 | convolution fusion | flops 8596226048 | bytes 40894468 | tf_op jit(solution)/shard_map/dot_general | solution.py:21
  273.7 0.0 copy-start.1
  273.7 1.6 copy.17
  275.3 0.0 copy-done.1
  275.4 2.1 fusion.37
  277.4 0.0 copy-start.2
  277.4 2.4 copy.13
  279.9 0.0 copy-done.2
  279.9 1.0 copy.15
Async XLA Ops:
  8.0 3.7 %copy-start.3 = (f32[512,256]{1,0:T(8,128)S(1)}, f32[512,256]{1,0:T(8,128)}, u32[]{:S(2)}) copy-start(f32[512,256]{1,0:T(8,128)} %param.6) | copy-start | bytes 1572868
  8.0 220.5 %all-reduce.2.cloned.1.call-start = ((), (), s32[]{:S(2)}) async-start(), calls=%async_computation | async-start | bytes 1048576 | tf_op jit(solution)/shard_map/psum | solution.py:44
  11.0 232.7 %copy-start = (bf16[1,4096,256]{1,2,0:T(8,128)(2,1)}, bf16[1,4096,256]{1,2,0:T(8,128)(2,1)S(1)}, u32[]{:S(2)}) copy-start(bf16[1,4096,256]{1,2,0:T(8,128)(2,1)S(1)} %copy.8) | copy-start | bytes 6291460
  12.8 231.0 %all-gather.3.cloned.1.call-start = ((), (), s32[]{:S(2)}) async-start(), calls=%async_computation.1 | async-start | bytes 17825792 | tf_op jit(solution)/shard_map/all_gather | solution.py:49
  273.7 1.7 copy-start.1
  277.4 2.4 copy-start.2
Sparse Core Ops, SparseCore 0:
  12.9 215.5 all-reduce.1
Sparse Core Ops, SparseCore 1:
  15.9 227.8 all-gather.2
where the time goes:
time: 289 us; the launch traced here: 288 us
  waiting for transfers between devices  226 us (78%)
  matrix products  29.9 us (10%)
  between operations  16.2 us (6%)
  local copies, waits for them, and re-layouts  11.6 us (4%)
  other arithmetic  4.87 us (2%)
    psum x1, waiting for transfers between devices, local(): summed = lax.psum(drift, 'replica')  214 us
    dot_general x1, matrix products, fold_rows(): lax.dot_general(shard_rows, residual, (((0,), (0,)), ((), ())), preferred...  29.9 us
    unnamed x15, local copies, waits for them, and re-layouts  11.6 us
    all_gather x1, waiting for transfers between devices, local(): lax.all_gather(batches[0], 'tensor', axis=0, tiled=True)  11.3 us
  transfers between devices with their start and end apart: 2, of which 2 were waited for; matrix products, arithmetic and copies ran while one was open for 2% of the time, Pallas kernels for 0%

commit v1 on v0

v1 whole, which is shorter than its diff:
```python
import functools
import math

import jax
import jax.numpy as jnp
from jax import lax
from jax.experimental import pallas as pl
from jax.experimental.pallas import tpu as pltpu
from jax.sharding import PartitionSpec as P

FRAGMENTS = 8
CHUNKS = 4
W_PIECES = 8
TILES = 8

inner_rate = 128.0
outer_rate = 0.7
nesterov_mu = 0.9

MESH = pl.DeviceIdType.MESH


def step_kernel(
    nz, total_rows, x_ref, w_ref, o_ref,
    xb, wv, acc, resid, stage,
    own_send, w_send, w_recv, got, ring_send, sib_send, out_send, out_recv,
):
    rows, width = x_ref.shape
    columns = w_ref.shape[1]
    chunk = rows // CHUNKS
    piece = width // W_PIECES
    tile = width // TILES
    inv_root = 1.0 / math.sqrt(width)

    rep = lax.axis_index("replica")
    ten = lax.axis_index("tensor")
    core = lax.rem(rep, 2)
    far = ten // nz
    z = lax.rem(ten, nz)
    ahead = lax.rem(z + 1 - 2 * core + nz, nz)
    behind = lax.rem(z - 1 + 2 * core + nz, nz)
    nxt = (rep, far * nz + ahead)
    prv = (rep, far * nz + behind)
    sibling = (rep + 1 - 2 * core, ten)
    partner = (rep + 1 - 2 * core, (1 - far) * nz + z)
    swapped = core + far == 1
    col_first = pl.multiple_of((core * nz + z) * columns, columns)
    mine = core * rows
    other = (1 - core) * rows

    barrier = pltpu.get_barrier_semaphore()
    for peer in (nxt, prv, sibling):
        pl.semaphore_signal(barrier, inc=1, device_id=peer, device_id_type=MESH)

    @pl.when(swapped)
    def _():
        pl.semaphore_signal(barrier, inc=1, device_id=partner, device_id_type=MESH)
        pl.semaphore_wait(barrier, 4)

    @pl.when(jnp.logical_not(swapped))
    def _():
        pl.semaphore_wait(barrier, 3)

    def remote(src, dst, send, recv, peer):
        return pltpu.make_async_remote_copy(
            src_ref=src, dst_ref=dst, send_sem=send, recv_sem=recv, device_id=peer, device_id_type=MESH
        )

    def x_over(j):
        return remote(
            x_ref.at[pl.ds(j * chunk, chunk)], xb.at[0, pl.ds(other + j * chunk, chunk)],
            own_send.at[j], got.at[0, 0, j], partner,
        )

    def w_over(k):
        return remote(
            w_ref.at[pl.ds(k * piece, piece)], wv.at[pl.ds(k * piece, piece)],
            w_send.at[k], w_recv.at[k], partner,
        )

    def x_here(j):
        return pltpu.make_async_copy(
            x_ref.at[pl.ds(j * chunk, chunk)], xb.at[0, pl.ds(mine + j * chunk, chunk)], got.at[0, 0, j]
        )

    def w_here(k):
        return pltpu.make_async_copy(
            w_ref.at[pl.ds(k * piece, piece)], wv.at[pl.ds(k * piece, piece)], w_recv.at[k]
        )

    @pl.when(swapped)
    def _():
        for j in range(CHUNKS):
            x_over(j).start()
        for k in range(W_PIECES):
            w_over(k).start()

    @pl.when(jnp.logical_not(swapped))
    def _():
        for j in range(CHUNKS):
            x_here(j).start()
        for k in range(W_PIECES):
            w_here(k).start()

    def arrived(s, lane, j):
        place = (mine if lane == 0 else other) + j * chunk
        ref = xb.at[s, pl.ds(place, chunk)]
        pltpu.make_async_copy(ref, ref, got.at[s, lane, j]).wait()

    def ring(s, j):
        place = pl.ds(mine + j * chunk, chunk)
        return remote(xb.at[s, place], xb.at[s + 1, place], ring_send.at[s, j], got.at[s + 1, 0, j], nxt)

    def share(s, j):
        place = pl.ds(mine + j * chunk, chunk)
        return remote(xb.at[s, place], xb.at[s, place], sib_send.at[s, j], got.at[s, 1, j], sibling)

    def pass_on(s, j, onward):
        arrived(s, 0, j)
        if onward:
            ring(s, j).start()
        share(s, j).start()

    def forward(s):
        for j in range(CHUNKS):
            arrived(s, 1, j)
        outputs = jnp.dot(xb[s], wv[...], preferred_element_type=jnp.float32) * inv_root
        target = xb[s, :, pl.ds(col_first, columns)].astype(jnp.float32)
        resid[...] = (outputs - target).astype(jnp.bfloat16)

    def grad_tile(s, t):
        return lax.dot_general(
            xb[s, :, pl.ds(t * tile, tile)], resid[...], (((0,), (0,)), ((), ())),
            preferred_element_type=jnp.float32,
        )

    def backward(s):
        @pl.loop(0, TILES)
        def _(t):
            t = pl.multiple_of(t * tile, tile)
            acc[pl.ds(t, tile), :] += lax.dot_general(
                xb[s, :, pl.ds(t, tile)], resid[...], (((0,), (0,)), ((), ())),
                preferred_element_type=jnp.float32,
            )

    acc[...] = jnp.zeros_like(acc)
    half = nz // 2

    def early(s, carry):
        for j in range(CHUNKS):
            pass_on(s, j, True)
        return carry

    lax.fori_loop(0, half, early, 0)

    for k in range(W_PIECES):
        ref = wv.at[pl.ds(k * piece, piece)]
        pltpu.make_async_copy(ref, ref, w_recv.at[k]).wait()

    def late(s, carry):
        first = 2 * (s - half)
        pass_on(s, 0, True)
        forward(first)
        pass_on(s, 1, True)
        backward(first)
        pass_on(s, 2, True)
        forward(first + 1)
        pass_on(s, 3, True)
        backward(first + 1)
        return carry

    lax.fori_loop(half, nz - 1, late, 0)

    last = nz - 1
    pass_on(last, 0, False)
    forward(last - 1)
    pass_on(last, 1, False)
    backward(last - 1)
    pass_on(last, 2, False)
    pass_on(last, 3, False)
    forward(last)

    def out_over(t):
        place = pl.ds(t * tile, tile)
        return remote(stage.at[place], o_ref.at[place], out_send.at[t], out_recv.at[t], partner)

    def out_here(t):
        place = pl.ds(t * tile, tile)
        return pltpu.make_async_copy(stage.at[place], o_ref.at[place], out_recv.at[t])

    for t in range(TILES):
        place = pl.ds(t * tile, tile)
        gradient = acc[place, :] + grad_tile(last, t)
        scaled = gradient * (inv_root / total_rows)
        stage[place, :] = (wv[place, :].astype(jnp.float32) - inner_rate * scaled).astype(jnp.bfloat16)

        @pl.when(swapped)
        def _():
            out_over(t).start()

        @pl.when(jnp.logical_not(swapped))
        def _():
            out_here(t).start()

    @pl.when(swapped)
    def _():
        for j in range(CHUNKS):
            x_over(j).wait_send()
        for k in range(W_PIECES):
            w_over(k).wait_send()
        for t in range(TILES):
            out_over(t).wait()

    @pl.when(jnp.logical_not(swapped))
    def _():
        for t in range(TILES):
            out_here(t).wait()

    def drain(s, carry):
        for j in range(CHUNKS):
            share(s, j).wait_send()
        return carry

    lax.fori_loop(0, nz, drain, 0)

    def drain_ring(s, carry):
        for j in range(CHUNKS):
            ring(s, j).wait_send()
        return carry

    lax.fori_loop(0, nz - 1, drain_ring, 0)


def inner_step(nz, tokens, weight):
    rows, width = tokens.shape
    columns = weight.shape[1]
    total_rows = rows * 2 * nz
    flops = 4 * total_rows * width * columns
    return pl.pallas_call(
        functools.partial(step_kernel, nz, total_rows),
        out_shape=jax.ShapeDtypeStruct((width, columns), jnp.bfloat16),
        in_specs=[pl.BlockSpec(memory_space=pl.ANY)] * 2,
        out_specs=pl.BlockSpec(memory_space=pl.ANY),
        scratch_shapes=[
            pltpu.VMEM((nz, 2 * rows, width), jnp.bfloat16),
            pltpu.VMEM((width, columns), jnp.bfloat16),
            pltpu.VMEM((width, columns), jnp.float32),
            pltpu.VMEM((2 * rows, columns), jnp.bfloat16),
            pltpu.VMEM((width, columns), jnp.bfloat16),
            pltpu.SemaphoreType.DMA((CHUNKS,)),
            pltpu.SemaphoreType.DMA((W_PIECES,)),
            pltpu.SemaphoreType.DMA((W_PIECES,)),
            pltpu.SemaphoreType.DMA((nz, 2, CHUNKS)),
            pltpu.SemaphoreType.DMA((nz - 1, CHUNKS)),
            pltpu.SemaphoreType.DMA((nz, CHUNKS)),
            pltpu.SemaphoreType.DMA((TILES,)),
            pltpu.SemaphoreType.DMA((TILES,)),
        ],
        cost_estimate=pl.CostEstimate(flops=flops, bytes_accessed=8 << 20, transcendentals=0),
        compiler_params=pltpu.CompilerParams(
            collective_id=0, has_side_effects=True, vmem_limit_bytes=48 << 20
        ),
    )(tokens, weight)


def local(nz, params, anchor, momentum, tokens, fragment):
    weight = params[0]
    width = weight.shape[0]
    frag_rows = width // FRAGMENTS
    first_row = fragment[0] * frag_rows
    before_rows = lax.dynamic_slice_in_dim(weight, first_row, frag_rows, 0).astype(jnp.float32)
    drift = anchor - before_rows
    summed = lax.psum(drift, "replica")
    outer_grad = summed / lax.axis_size("replica")
    momentum_out = nesterov_mu * momentum + outer_grad
    anchor_out = anchor - outer_rate * (outer_grad + nesterov_mu * momentum_out)
    after = inner_step(nz, tokens[0, 0], weight)
    after_rows = lax.dynamic_slice_in_dim(after, first_row, frag_rows, 0).astype(jnp.float32)
    merged = (anchor_out + (after_rows - before_rows)).astype(jnp.bfloat16)
    params_out = lax.dynamic_update_slice_in_dim(after, merged, first_row, 0)
    return (params_out[None], momentum_out, anchor_out)


def solution(mesh):
    return jax.shard_map(
        functools.partial(local, mesh.shape["tensor"] // 2),
        mesh=mesh,
        in_specs=(
            P("replica", None, "tensor"),
            P(None, "tensor"),
            P(None, "tensor"),
            P("replica", None, "tensor", None),
            P(),
        ),
        out_specs=(P("replica", None, "tensor"), P(None, "tensor"), P(None, "tensor")),
        check_vma=False,
    )
```

time: 289 us -> 150 us (0.52)
  waiting for transfers between devices: 226 us -> 0.02 us
  Pallas kernels: 0 us -> 126 us
  matrix products: 29.9 us -> 0 us
  local copies, waits for them, and re-layouts: 11.6 us -> 4.68 us
    psum x1, waiting for transfers between devices: 214 us -> 0.01 us  [local(): summed = lax.psum(drift, 'replica')]
    pallas_call x0 -> x1, Pallas kernels: none -> 126 us  [inner_step(): pl.pallas_call(functools.partial(step_kernel, nz, total_rows), out_shape=...]
    dot_general x1 -> x0, matrix products: 29.9 us -> none  [fold_rows(): lax.dot_general(shard_rows, residual, (((0,), (0,)), ((), ())), preferred...]
    all_gather x1 -> x0, waiting for transfers between devices: 11.3 us -> none  [local(): lax.all_gather(batches[0], 'tensor', axis=0, tiled=True)]
    unnamed x15 -> x9, local copies, waits for them, and re-layouts: 11.6 us -> 4.68 us
  transfers between devices with their start and end apart: 2 -> 1, of which waited for: 2 -> 0; matrix products, arithmetic and copies ran while one was open for 2% -> 1% of each run, Pallas kernels for 0% -> 84%
where the time goes in v1:
time: 150 us
  Pallas kernels  126 us (84%)
  between operations  14.7 us (10%)
  local copies, waits for them, and re-layouts  4.68 us (3%)
  other arithmetic  4.28 us (3%)
    pallas_call x1, Pallas kernels, inner_step(): pl.pallas_call(functools.partial(step_kernel, nz, total_rows), out_shape=...  126 us
    unnamed x9, local copies, waits for them, and re-layouts  4.68 us
  transfers between devices with their start and end apart: 1, of which 0 were waited for; matrix products, arithmetic and copies ran while one was open for 1% of the time, Pallas kernels for 84%

profile of v1, /device:TPU:1, one launch (start us, length us, event | category | flops | bytes accessed | tf_op | source)
XLA Modules:
  0.0 149.7 jit_solution(14198214574533608117)
XLA Ops:
  7.2 0.0 all-reduce.2.cloned.1.call-start
  7.9 2.0 %convert_subtract_fusion.1 = f32[512,256]{1,0:T(8,128)} fusion(f32[512,256]{1,0:T(8,128)} %param.6, bf16[1,4096,256]{2,1,0:T(8,128)(2,1)} %param.5, s32[]{:T(128)S(6)} %select_n.2), kind=kLoop, calls=%fused_computation.1 | loop fusion | flops 262144 | bytes 1310724 | tf_op jit(solution)/shard_map/sub | solution.py:272
  9.8 0.0 all-reduce.2.cloned.1.call-update
  9.8 0.0 copy-start
  9.9 1.6 %copy-done = bf16[1,4096,256]{2,1,0:T(8,128)(2,1)S(1)} copy-done((bf16[1,4096,256]{2,1,0:T(8,128)(2,1)S(1)}, bf16[1,4096,256]{2,1,0:T(8,128)(2,1)}, u32[]{:S(2)}) %copy-start) | copy-done | bytes 2097176
  11.4 0.0 copy-start.1
  11.4 1.2 copy-done.1
  12.7 126.0 %shard_map.76 = bf16[4096,256]{1,0:T(8,128)(2,1)S(1)} custom-call(bf16[128,4096]{1,0:T(8,128)(2,1)S(1)} %bitcast.14, bf16[4096,256]{1,0:T(8,128)(2,1)S(1)} %bitcast.13), custom_call_target="tpu_custom_call" | custom-call | flops 8589934592 | bytes 8388608 | tf_op jit(solution)/shard_map/pallas_call | solution.py:239
  138.6 0.0 copy-start.2
  138.6 0.0 copy-start.3
  138.7 1.3 copy.9
  140.0 0.0 all-reduce.2.cloned.1.call-done
  140.0 0.0 copy-done.2
  140.0 0.5 copy-done.3
  140.5 2.3 %fusion.3 = (bf16[1,4096,256]{2,1,0:T(8,128)(2,1)}, f32[512,256]{1,0:T(8,128)}, f32[512,256]{1,0:T(8,128)}) fusion(bf16[1,4096,256]{2,1,0:T(8,128)(2,1)} %copy.9, s32[]{:T(128)S(6)} %select_n.2, bf16[4096,256]{1,0:T(8,128)(2,1)S(1)} %shard_map.76, bf16[1,4096,256]{2,1,0:T(8,128)(2,1)} %param.5, f32[512,256]{1,0:T(8,128)S(1)} %copy-done.2, ...), kind=kLoop, calls=%fused_computation.7 | loop fusion | flops 1572864 | bytes 3407876 | tf_op jit(solution)/shard_map/dynamic_update_slice | solution.py:280
Async XLA Ops:
  7.2 132.8 %all-reduce.2.cloned.1.call-start = ((), (), s32[]{:S(2)}) async-start(), calls=%async_computation | async-start | bytes 1048576 | tf_op jit(solution)/shard_map/psum | solution.py:273
  9.8 1.6 %copy-start = (bf16[1,4096,256]{2,1,0:T(8,128)(2,1)S(1)}, bf16[1,4096,256]{2,1,0:T(8,128)(2,1)}, u32[]{:S(2)}) copy-start(bf16[1,4096,256]{2,1,0:T(8,128)(2,1)} %param.5) | copy-start | bytes 6291460
  11.4 1.2 copy-start.1
  138.6 1.4 copy-start.2
  138.6 1.9 %copy-start.3 = (f32[512,256]{1,0:T(8,128)S(1)}, f32[512,256]{1,0:T(8,128)}, u32[]{:S(2)}) copy-start(f32[512,256]{1,0:T(8,128)} %param.7) | copy-start | bytes 1572868
Sparse Core Ops, SparseCore 0:
  11.2 128.5 all-reduce.1

commit v2 on v1

v2 whole, which is shorter than its diff:
```python
import functools
import math

import jax
import jax.numpy as jnp
from jax import lax
from jax.experimental import pallas as pl
from jax.experimental.pallas import tpu as pltpu
from jax.sharding import PartitionSpec as P

LATE_ROWS = 16
PARTS = (2, 3, 1, 1)
CHUNKS = len(PARTS)
W_PIECES = 8
TILES = 8

inner_rate = 128.0
outer_rate = 0.7
nesterov_mu = 0.9

MESH = pl.DeviceIdType.MESH


def step_kernel(
    nz, ny, total_rows, frag_ref, x_ref, w_ref, a_ref, m_ref, o_ref, mo_ref, ao_ref,
    xb, xq, wv, home, acc, resid, resid_late, stage, relay, back, fin,
    anchor, momentum, frag_out, frag_in, part, from_x, from_y, grad,
    own_send, w_send, w_recv, got, ring_send, sib_send, out_send, relay_recv, relay_send, back_recv,
    q_own, mate_send, mate_recv, q_send, q_recv, fin_sem, load_sem, store_sem,
    a_send, a_recv, b_send, b_recv, c_send, c_recv, d_send, d_recv, e_send, e_recv, f_send, f_recv,
):
    shard, width = x_ref.shape
    rows = shard - LATE_ROWS
    columns = w_ref.shape[1]
    sizes = [rows * part // 7 for part in PARTS]
    starts = [sum(sizes[:j]) for j in range(CHUNKS)]
    piece = width // W_PIECES
    tile = width // TILES
    inv_root = 1.0 / math.sqrt(width)

    rep = lax.axis_index("replica")
    ten = lax.axis_index("tensor")
    core = lax.rem(rep, 2)
    far = ten // nz
    z = lax.rem(ten, nz)
    up = (rep, far * nz + lax.rem(z + 1, nz))
    down = (rep, far * nz + lax.rem(z + nz - 1, nz))
    sibling = (rep + 1 - 2 * core, ten)
    partner = (rep + 1 - 2 * core, (1 - far) * nz + z)
    mate = (rep, (1 - far) * nz + z)
    ends = (
        (rep, far * nz + lax.rem(z + 1 - 2 * core + nz, nz)),
        (rep, far * nz + lax.rem(z - 1 + 2 * core + nz, nz)),
    )
    swapped = core + far == 1
    near = rep // (2 * ny)
    y = lax.rem(rep // 2, ny)
    across = (lax.rem(rep + 2 * ny, 4 * ny), ten)
    along = [((near * ny + lax.rem(y + d, ny)) * 2 + core, ten) for d in range(1, ny)]
    frag_rows = a_ref.shape[0]
    half_rows = frag_rows // 2
    quarter_rows = frag_rows // 4
    piece_rows = quarter_rows // ny
    half_first = core * half_rows
    quarter_first = half_first + near * quarter_rows
    piece_first = quarter_first + y * piece_rows
    col_first = pl.multiple_of((core * nz + z) * columns, columns)
    col_home = pl.multiple_of(ten * columns, columns)
    mine = core * rows
    other = (1 - core) * rows

    barrier = pltpu.get_barrier_semaphore()
    for peer in (up, down, sibling, mate, across, *along):
        pl.semaphore_signal(barrier, inc=1, device_id=peer, device_id_type=MESH)

    @pl.when(swapped)
    def _():
        pl.semaphore_signal(barrier, inc=1, device_id=partner, device_id_type=MESH)
        pl.semaphore_wait(barrier, 5 + ny)

    @pl.when(jnp.logical_not(swapped))
    def _():
        pl.semaphore_wait(barrier, 4 + ny)

    def remote(src, dst, send, recv, peer):
        return pltpu.make_async_remote_copy(
            src_ref=src, dst_ref=dst, send_sem=send, recv_sem=recv, device_id=peer, device_id_type=MESH
        )

    def x_over(j):
        return remote(
            x_ref.at[pl.ds(starts[j], sizes[j])], xb.at[0, pl.ds(other + starts[j], sizes[j])],
            own_send.at[j], got.at[0, 0, j], partner,
        )

    def w_over(k):
        return remote(
            w_ref.at[pl.ds(k * piece, piece)], wv.at[pl.ds(k * piece, piece)],
            w_send.at[k], w_recv.at[k], partner,
        )

    def x_here(j):
        return pltpu.make_async_copy(
            x_ref.at[pl.ds(starts[j], sizes[j])], xb.at[0, pl.ds(mine + starts[j], sizes[j])], got.at[0, 0, j]
        )

    def w_here(k):
        return pltpu.make_async_copy(
            w_ref.at[pl.ds(k * piece, piece)], wv.at[pl.ds(k * piece, piece)], w_recv.at[k]
        )

    late_src = x_ref.at[pl.ds(rows, LATE_ROWS)]

    def late_at(lane, step, way):
        offset = (nz - step) % nz if way == 0 else step
        return xq.at[pl.ds((lane * nz + offset) * LATE_ROWS, LATE_ROWS)]

    late_here = pltpu.make_async_copy(late_src, late_at(0, 0, 0), q_own)
    late_mate = remote(late_src, late_at(1, 0, 0), mate_send, mate_recv, mate)

    @pl.when(swapped)
    def _():
        for j in range(CHUNKS):
            x_over(j).start()

    late_here.start()
    late_mate.start()

    @pl.when(swapped)
    def _():
        for k in range(W_PIECES):
            w_over(k).start()

    @pl.when(jnp.logical_not(swapped))
    def _():
        for j in range(CHUNKS):
            x_here(j).start()
        for k in range(W_PIECES):
            w_here(k).start()

    loads = [
        pltpu.make_async_copy(src, dst, load_sem.at[k])
        for k, (src, dst) in enumerate(((w_ref, home), (a_ref, anchor), (m_ref, momentum)))
    ]
    for copy in loads:
        copy.start()

    def arrived(s, lane, j):
        place = (mine if lane == 0 else other) + starts[j]
        ref = xb.at[s, pl.ds(place, sizes[j])]
        pltpu.make_async_copy(ref, ref, got.at[s, lane, j]).wait()

    def ring(s, j):
        place = pl.ds(mine + starts[j], sizes[j])
        end = ends[0 if j in (0, CHUNKS - 1) else 1]
        return remote(xb.at[s, place], xb.at[s + 1, place], ring_send.at[s, j], got.at[s + 1, 0, j], end)

    def share(s, j):
        place = pl.ds(mine + starts[j], sizes[j])
        return remote(xb.at[s, place], xb.at[s, place], sib_send.at[s, j], got.at[s, 1, j], sibling)

    def pass_on(s, j, onward):
        arrived(s, 0, j)
        if onward:
            ring(s, j).start()
        share(s, j).start()

    def forward(s):
        for j in range(CHUNKS):
            arrived(s, 1, j)
        outputs = jnp.dot(xb[s], wv[...], preferred_element_type=jnp.float32) * inv_root
        target = xb[s, :, pl.ds(col_first, columns)].astype(jnp.float32)
        resid[...] = (outputs - target).astype(jnp.bfloat16)

    def grad_tile(s, t):
        return lax.dot_general(
            xb[s, :, pl.ds(t * tile, tile)], resid[...], (((0,), (0,)), ((), ())),
            preferred_element_type=jnp.float32,
        )

    def backward(s):
        @pl.loop(0, TILES)
        def _(t):
            t = pl.multiple_of(t * tile, tile)
            acc[pl.ds(t, tile), :] += lax.dot_general(
                xb[s, :, pl.ds(t, tile)], resid[...], (((0,), (0,)), ((), ())),
                preferred_element_type=jnp.float32,
            )

    over_core = remote(
        frag_out.at[pl.ds((1 - core) * half_rows, half_rows)], frag_in, a_send, a_recv, sibling
    )
    over_x = remote(
        part.at[pl.ds((1 - near) * quarter_rows, quarter_rows)], from_x, b_send, b_recv, across
    )
    over_y = [
        remote(
            part.at[pl.ds(near * quarter_rows + lax.rem(y + d, ny) * piece_rows, piece_rows)],
            from_y.at[d - 1], c_send.at[d - 1], c_recv.at[d - 1], along[d - 1],
        )
        for d in range(1, ny)
    ]
    piece_at = grad.at[pl.ds(piece_first, piece_rows)]
    quarter_at = grad.at[pl.ds(quarter_first, quarter_rows)]
    half_at = grad.at[pl.ds(half_first, half_rows)]
    back_y = [
        remote(piece_at, piece_at, d_send.at[d - 1], d_recv.at[d - 1], along[d - 1]) for d in range(1, ny)
    ]
    back_x = remote(quarter_at, quarter_at, e_send, e_recv, across)
    back_core = remote(half_at, half_at, f_send, f_recv, sibling)

    def chosen(k):
        return jnp.full((frag_rows, columns), frag_ref[0], jnp.int32) == k

    def sum_core():
        for copy in loads:
            copy.wait()
        rows_of = home[pl.ds(0, frag_rows), :].astype(jnp.float32)
        for k in range(1, width // frag_rows):
            block = home[pl.ds(k * frag_rows, frag_rows), :].astype(jnp.float32)
            rows_of = jnp.where(chosen(k), block, rows_of)
        frag_out[...] = rows_of.astype(jnp.bfloat16)
        over_core.start()

    def sum_x():
        over_core.wait()
        fixed = anchor[pl.ds(half_first, half_rows), :]
        own = frag_out[pl.ds(half_first, half_rows), :].astype(jnp.float32)
        part[...] = (fixed - own) + (fixed - frag_in[...].astype(jnp.float32))
        over_x.start()

    def sum_y():
        over_x.wait()
        part[pl.ds(near * quarter_rows, quarter_rows), :] += from_x[...]
        for copy in over_y:
            copy.start()

    def gather_y():
        for copy in over_y:
            copy.wait()
        total = part[pl.ds(near * quarter_rows + y * piece_rows, piece_rows), :]
        for d in range(1, ny):
            total += from_y[d - 1]
        grad[pl.ds(piece_first, piece_rows), :] = total / (4 * ny)
        for copy in back_y:
            copy.start()

    def gather_x():
        for copy in back_y:
            copy.wait()
        back_x.start()

    def gather_core():
        back_x.wait()
        back_core.start()

    stores = [
        pltpu.make_async_copy(src, dst, store_sem.at[k])
        for k, (src, dst) in enumerate(((momentum, mo_ref), (anchor, ao_ref)))
    ]

    def outer_step():
        back_core.wait()
        outer_grad = grad[...]
        moved = nesterov_mu * momentum[...] + outer_grad
        momentum[...] = moved
        anchor[...] = anchor[...] - outer_rate * (outer_grad + nesterov_mu * moved)
        for copy in stores:
            copy.start()

    def outer_stage(s):
        for k, stage_of in enumerate((sum_core, sum_x, sum_y, gather_y, gather_x, gather_core, outer_step)):
            pl.when(s == k)(stage_of)

    acc[...] = jnp.zeros_like(acc)
    half = nz // 2

    def early(s, carry):
        for j in range(CHUNKS):
            pass_on(s, j, True)
        outer_stage(s)
        return carry

    lax.fori_loop(0, half, early, 0)

    for k in range(W_PIECES):
        ref = wv.at[pl.ds(k * piece, piece)]
        pltpu.make_async_copy(ref, ref, w_recv.at[k]).wait()

    def late(s, carry):
        first = 2 * (s - half)
        pass_on(s, 0, True)
        forward(first)
        pass_on(s, 1, True)
        backward(first)
        pass_on(s, 2, True)
        forward(first + 1)
        pass_on(s, 3, True)
        backward(first + 1)
        outer_stage(s)
        return carry

    lax.fori_loop(half, nz - 1, late, 0)

    lanes = [(lane, way, half if lane == way else half - 1) for lane in range(2) for way in range(2)]

    def late_send(lane, step, way):
        return remote(
            late_at(lane, step - 1, way), late_at(lane, step, way),
            q_send.at[lane, way, step - 1], q_recv.at[lane, way, step - 1], (up, down)[way],
        )

    late_here.wait()
    late_mate.wait()
    for lane, way, most in lanes:
        late_send(lane, 1, way).start()

    last = nz - 1
    pass_on(last, 0, False)
    forward(last - 1)
    pass_on(last, 1, False)
    backward(last - 1)
    pass_on(last, 2, False)
    pass_on(last, 3, False)
    forward(last)

    def tile_at(t):
        return pl.ds(t * tile, tile)

    def relay_at(t):
        return relay.at[pl.ds(t // 2 * tile, tile)]

    def back_over(t):
        if t % 2 == 0:
            return remote(stage.at[tile_at(t)], back.at[tile_at(t)], out_send.at[t], back_recv.at[t], partner)
        return remote(stage.at[tile_at(t)], relay_at(t), out_send.at[t], relay_recv.at[t // 2], sibling)

    def back_relay(t):
        return remote(relay_at(t), back.at[tile_at(t)], relay_send.at[t // 2], back_recv.at[t], mate)

    @pl.when(swapped)
    def _():
        for t in range(TILES):
            stage[tile_at(t), :] = (acc[tile_at(t), :] + grad_tile(last, t)).astype(jnp.bfloat16)
            back_over(t).start()

    @pl.when(jnp.logical_not(swapped))
    def _():
        for t in range(TILES):
            acc[tile_at(t), :] += grad_tile(last, t)
            if t % 2 == 1:
                ref = relay_at(t)
                pltpu.make_async_copy(ref, ref, relay_recv.at[t // 2]).wait()
                back_relay(t).start()

    for step in range(1, half + 1):
        for lane, way, most in lanes:
            if step <= most:
                late_send(lane, step, way).wait_recv()
            if step < most:
                late_send(lane, step + 1, way).start()

    outputs = jnp.dot(xq[...], home[...], preferred_element_type=jnp.float32) * inv_root
    target = xq[:, pl.ds(col_home, columns)].astype(jnp.float32)
    resid_late[...] = (outputs - target).astype(jnp.bfloat16)

    def out_here(t):
        return pltpu.make_async_copy(fin.at[tile_at(t)], o_ref.at[tile_at(t)], fin_sem.at[t])

    for t in range(TILES):
        place = tile_at(t)

        @pl.when(swapped)
        def _():
            ref = back.at[place]
            pltpu.make_async_copy(ref, ref, back_recv.at[t]).wait()
            acc[place, :] = back[place, :].astype(jnp.float32)

        gradient = acc[place, :] + lax.dot_general(
            xq[:, place], resid_late[...], (((0,), (0,)), ((), ())), preferred_element_type=jnp.float32
        )
        scaled = gradient * (inv_root / total_rows)
        before = home[place, :].astype(jnp.float32)
        after = (before - inner_rate * scaled).astype(jnp.bfloat16).astype(jnp.float32)
        merged = anchor[...] + (after - before)
        fin[place, :] = jnp.where(chosen(t), merged, after).astype(jnp.bfloat16)
        out_here(t).start()

    @pl.when(swapped)
    def _():
        for j in range(CHUNKS):
            x_over(j).wait_send()
        for k in range(W_PIECES):
            w_over(k).wait_send()
        for t in range(TILES):
            back_over(t).wait_send()

    @pl.when(jnp.logical_not(swapped))
    def _():
        for t in range(1, TILES, 2):
            back_relay(t).wait_send()

    for lane, way, most in lanes:
        for step in range(1, most + 1):
            late_send(lane, step, way).wait_send()
    for t in range(TILES):
        out_here(t).wait()
    for copy in stores:
        copy.wait()

    def drain(s, carry):
        for j in range(CHUNKS):
            share(s, j).wait_send()
        return carry

    lax.fori_loop(0, nz, drain, 0)

    def drain_ring(s, carry):
        for j in range(CHUNKS):
            ring(s, j).wait_send()
        return carry

    lax.fori_loop(0, nz - 1, drain_ring, 0)


def window(nz, ny, fragment, tokens, weight, anchor, momentum):
    rows, width = tokens.shape
    columns = weight.shape[1]
    frag_rows = anchor.shape[0]
    total_rows = rows * 2 * nz
    flops = 4 * total_rows * width * columns
    whole = pl.BlockSpec(memory_space=pltpu.HBM)
    result = pl.BlockSpec(memory_space=pl.ANY)
    dma = pltpu.SemaphoreType.DMA
    return pl.pallas_call(
        functools.partial(step_kernel, nz, ny, total_rows),
        out_shape=(
            jax.ShapeDtypeStruct((width, columns), jnp.bfloat16),
            jax.ShapeDtypeStruct(momentum.shape, jnp.float32),
            jax.ShapeDtypeStruct(anchor.shape, jnp.float32),
        ),
        in_specs=[pl.BlockSpec(memory_space=pltpu.SMEM), whole, whole, whole, whole],
        out_specs=(result, result, result),
        scratch_shapes=[
            pltpu.VMEM((nz, 2 * (rows - LATE_ROWS), width), jnp.bfloat16),
            pltpu.VMEM((2 * nz * LATE_ROWS, width), jnp.bfloat16),
            pltpu.VMEM((width, columns), jnp.bfloat16),
            pltpu.VMEM((width, columns), jnp.bfloat16),
            pltpu.VMEM((width, columns), jnp.float32),
            pltpu.VMEM((2 * (rows - LATE_ROWS), columns), jnp.bfloat16),
            pltpu.VMEM((2 * nz * LATE_ROWS, columns), jnp.bfloat16),
            pltpu.VMEM((width, columns), jnp.bfloat16),
            pltpu.VMEM((width // 2, columns), jnp.bfloat16),
            pltpu.VMEM((width, columns), jnp.bfloat16),
            pltpu.VMEM((width, columns), jnp.bfloat16),
            pltpu.VMEM((frag_rows, columns), jnp.float32),
            pltpu.VMEM((frag_rows, columns), jnp.float32),
            pltpu.VMEM((frag_rows, columns), jnp.bfloat16),
            pltpu.VMEM((frag_rows // 2, columns), jnp.bfloat16),
            pltpu.VMEM((frag_rows // 2, columns), jnp.float32),
            pltpu.VMEM((frag_rows // 4, columns), jnp.float32),
            pltpu.VMEM((ny - 1, frag_rows // (4 * ny), columns), jnp.float32),
            pltpu.VMEM((frag_rows, columns), jnp.float32),
            dma((CHUNKS,)), dma((W_PIECES,)), dma((W_PIECES,)), dma((nz, 2, CHUNKS)), dma((nz - 1, CHUNKS)),
            dma((nz, CHUNKS)), dma((TILES,)), dma((TILES // 2,)), dma((TILES // 2,)), dma((TILES,)),
            dma, dma, dma, dma((2, 2, nz // 2)), dma((2, 2, nz // 2)), dma((TILES,)), dma((3,)), dma((2,)),
            dma, dma, dma, dma, dma((ny - 1,)), dma((ny - 1,)), dma((ny - 1,)), dma((ny - 1,)), dma, dma, dma, dma,
        ],
        cost_estimate=pl.CostEstimate(flops=flops, bytes_accessed=8 << 20, transcendentals=0),
        compiler_params=pltpu.CompilerParams(
            collective_id=0, has_side_effects=True, vmem_limit_bytes=54 << 20
        ),
    )(fragment, tokens, weight, anchor, momentum)


def local(nz, ny, params, anchor, momentum, tokens, fragment):
    params_out, momentum_out, anchor_out = window(
        nz, ny, fragment, tokens[0, 0], params[0], anchor, momentum
    )
    return (params_out[None], momentum_out, anchor_out)


def solution(mesh):
    return jax.shard_map(
        functools.partial(local, mesh.shape["tensor"] // 2, mesh.shape["replica"] // 4),
        mesh=mesh,
        in_specs=(
            P("replica", None, "tensor"),
            P(None, "tensor"),
            P(None, "tensor"),
            P("replica", None, "tensor", None),
            P(),
        ),
        out_specs=(P("replica", None, "tensor"), P(None, "tensor"), P(None, "tensor")),
        check_vma=False,
    )
```

time: 150 us -> 124 us (0.83)
  between operations: 14.7 us -> 1.3 us
  Pallas kernels: 126 us -> 117 us
  other arithmetic: 4.28 us -> 0 us
    pallas_call x1, Pallas kernels: 126 us -> 117 us  [window(): pl.pallas_call(functools.partial(step_kernel, nz, ny, total_rows), out_sh...]
    dynamic_update_slice x1 -> x0, other arithmetic: 2.32 us -> none  [local(): params_out = lax.dynamic_update_slice_in_dim(after, merged, first_row, 0)]
    sub x1 -> x0, other arithmetic: 1.96 us -> none  [local(): drift = anchor - before_rows]
    unnamed x9 -> x7, local copies, waits for them, and re-layouts: 4.68 us -> 4.73 us
  transfers between devices with their start and end apart: 1 -> 0, of which waited for: 0 -> 0; matrix products, arithmetic and copies ran while one was open for 1% -> 0% of each run, Pallas kernels for 84% -> 0%
where the time goes in v2:
time: 124 us; the launch traced here: 123 us
  Pallas kernels  117 us (94%)
  local copies, waits for them, and re-layouts  4.73 us (4%)
  between operations  1.3 us (1%)
    pallas_call x1, Pallas kernels, window(): pl.pallas_call(functools.partial(step_kernel, nz, ny, total_rows), out_sh...  117 us
    unnamed x7, local copies, waits for them, and re-layouts  4.73 us

profile of v2, /device:TPU:1, one launch (start us, length us, event | category | flops | bytes accessed | tf_op | source)
XLA Modules:
  0.0 123.5 jit_solution(16260635174161709728)
XLA Ops:
  1.3 117.4 %shard_map.76 = (bf16[4096,256]{1,0:T(8,128)(2,1)}, f32[512,256]{1,0:T(8,128)}, f32[512,256]{1,0:T(8,128)}) custom-call(s32[1]{0:T(128)S(6)} %copy.11.frag_ref, bf16[128,4096]{1,0:T(8,128)(2,1)} %bitcast.5, bf16[4096,256]{1,0:T(8,128)(2,1)} %bitcast.4, f32[512,256]{1,0:T(8,128)} %a_ref.1, f32[512,256]{1,0:T(8,128)} %m_ref.1), custom_call_target="tpu_custom_call" | custom-call | flops 8589934592 | bytes 8388608 | tf_op jit(solution)/shard_map/pallas_call | solution.py:435
  118.7 0.0 copy-start.1
  118.7 0.0 copy-start
  118.7 3.1 %copy.12 = bf16[1,4096,256]{2,1,0:T(8,128)(2,1)} copy(bf16[1,4096,256]{2,1,0:T(8,128)(2,1)} %bitcast.3) | data formatting | bytes 4194304
  121.9 0.0 copy-done.1
  121.9 0.8 copy.13
  122.7 0.0 copy-done
  122.7 0.8 copy.14
Async XLA Ops:
  118.7 3.2 %copy-start.1 = (f32[512,256]{1,0:T(8,128)S(1)}, f32[512,256]{1,0:T(8,128)}, u32[]{:S(2)}) copy-start(f32[512,256]{1,0:T(8,128)} %get-tuple-element.13) | copy-start | bytes 1572868
  118.7 3.9 %copy-start = (f32[512,256]{1,0:T(8,128)S(1)}, f32[512,256]{1,0:T(8,128)}, u32[]{:S(2)}) copy-start(f32[512,256]{1,0:T(8,128)} %get-tuple-element.14) | copy-start | bytes 1572868

commit v3 on v2

--- a/solution.py
+++ b/solution.py
@@ -9,7 +9,7 @@
 from jax.sharding import PartitionSpec as P
 
 LATE_ROWS = 16
-PARTS = (2, 3, 1, 1)
+PARTS = (2, 2, 2, 1)
 CHUNKS = len(PARTS)
 W_PIECES = 8
 TILES = 8
@@ -435,9 +435,9 @@
     return pl.pallas_call(
         functools.partial(step_kernel, nz, ny, total_rows),
         out_shape=(
-            jax.ShapeDtypeStruct((width, columns), jnp.bfloat16),
-            jax.ShapeDtypeStruct(momentum.shape, jnp.float32),
-            jax.ShapeDtypeStruct(anchor.shape, jnp.float32),
+            pltpu.VMEM((width, columns), jnp.bfloat16),
+            pltpu.VMEM(momentum.shape, jnp.float32),
+            pltpu.VMEM(anchor.shape, jnp.float32),
         ),
         in_specs=[pl.BlockSpec(memory_space=pltpu.SMEM), whole, whole, whole, whole],
         out_specs=(result, result, result),
@@ -468,7 +468,7 @@
         ],
         cost_estimate=pl.CostEstimate(flops=flops, bytes_accessed=8 << 20, transcendentals=0),
         compiler_params=pltpu.CompilerParams(
-            collective_id=0, has_side_effects=True, vmem_limit_bytes=54 << 20
+            collective_id=0, has_side_effects=True, vmem_limit_bytes=59 << 20
         ),
     )(fragment, tokens, weight, anchor, momentum)
 

time: 124 us -> 119 us (0.960)
  Pallas kernels: 117 us -> 115 us
  local copies, waits for them, and re-layouts: 4.73 us -> 2.91 us
    pallas_call x1, Pallas kernels: 117 us -> 115 us  [window(): pl.pallas_call(functools.partial(step_kernel, nz, ny, total_rows), out_sh...]
    unnamed x7 -> x3, local copies, waits for them, and re-layouts: 4.73 us -> 2.91 us
where the time goes in v3:
time: 119 us
  Pallas kernels  115 us (97%)
  local copies, waits for them, and re-layouts  2.91 us (2%)
  between operations  1.29 us (1%)
    pallas_call x1, Pallas kernels, window(): pl.pallas_call(functools.partial(step_kernel, nz, ny, total_rows), out_sh...  115 us
    unnamed x3, local copies, waits for them, and re-layouts  2.91 us

profile of v3, /device:TPU:1, one launch (start us, length us, event | category | flops | bytes accessed | tf_op | source)
XLA Modules:
  0.0 119.3 jit_solution(16326775807869872709)
XLA Ops:
  1.3 115.1 %shard_map.76 = (bf16[4096,256]{1,0:T(8,128)(2,1)S(1)}, f32[512,256]{1,0:T(8,128)S(1)}, f32[512,256]{1,0:T(8,128)S(1)}) custom-call(s32[1]{0:T(128)S(6)} %copy.14.frag_ref, bf16[128,4096]{1,0:T(8,128)(2,1)} %bitcast.5, bf16[4096,256]{1,0:T(8,128)(2,1)} %bitcast.4, f32[512,256]{1,0:T(8,128)} %a_ref.1, f32[512,256]{1,0:T(8,128)} %m_ref.1), custom_call_target="tpu_custom_call" | custom-call | flops 8589934592 | bytes 8388608 | tf_op jit(solution)/shard_map/pallas_call | solution.py:435
  116.4 1.3 %copy.11 = bf16[1,4096,256]{2,1,0:T(8,128)(2,1)} copy(bf16[1,4096,256]{2,1,0:T(8,128)(2,1)S(1)} %bitcast.3) | data formatting | bytes 4194304
  117.7 0.8 copy.12
  118.5 0.8 copy.13

commit v4 on v3

--- a/solution.py
+++ b/solution.py
@@ -8,8 +8,7 @@
 from jax.experimental.pallas import tpu as pltpu
 from jax.sharding import PartitionSpec as P
 
-LATE_ROWS = 16
-PARTS = (2, 2, 2, 1)
+PARTS = (3, 1, 3, 1)
 CHUNKS = len(PARTS)
 W_PIECES = 8
 TILES = 8
@@ -23,16 +22,17 @@
 
 def step_kernel(
     nz, ny, total_rows, frag_ref, x_ref, w_ref, a_ref, m_ref, o_ref, mo_ref, ao_ref,
-    xb, xq, wv, home, acc, resid, resid_late, stage, relay, back, fin,
+    xb, xq, xm, wv, home, acc, resid, resid_late, stage, relay, back, fin,
     anchor, momentum, frag_out, frag_in, part, from_x, from_y, grad,
     own_send, w_send, w_recv, got, ring_send, sib_send, out_send, relay_recv, relay_send, back_recv,
-    q_own, mate_send, mate_recv, q_send, q_recv, fin_sem, load_sem, store_sem,
+    mate_send, mate_recv, q_send, q_recv, fin_sem, load_sem, store_sem,
     a_send, a_recv, b_send, b_recv, c_send, c_recv, d_send, d_recv, e_send, e_recv, f_send, f_recv,
 ):
-    shard, width = x_ref.shape
-    rows = shard - LATE_ROWS
+    rows, width = x_ref.shape
+    side = rows // 2
+    last = nz - 2
     columns = w_ref.shape[1]
-    sizes = [rows * part // 7 for part in PARTS]
+    sizes = [rows * part // 8 for part in PARTS]
     starts = [sum(sizes[:j]) for j in range(CHUNKS)]
     piece = width // W_PIECES
     tile = width // TILES
@@ -48,10 +48,6 @@
     sibling = (rep + 1 - 2 * core, ten)
     partner = (rep + 1 - 2 * core, (1 - far) * nz + z)
     mate = (rep, (1 - far) * nz + z)
-    ends = (
-        (rep, far * nz + lax.rem(z + 1 - 2 * core + nz, nz)),
-        (rep, far * nz + lax.rem(z - 1 + 2 * core + nz, nz)),
-    )
     swapped = core + far == 1
     near = rep // (2 * ny)
     y = lax.rem(rep // 2, ny)
@@ -109,22 +105,12 @@
             w_ref.at[pl.ds(k * piece, piece)], wv.at[pl.ds(k * piece, piece)], w_recv.at[k]
         )
 
-    late_src = x_ref.at[pl.ds(rows, LATE_ROWS)]
-
-    def late_at(lane, step, way):
-        offset = (nz - step) % nz if way == 0 else step
-        return xq.at[pl.ds((lane * nz + offset) * LATE_ROWS, LATE_ROWS)]
-
-    late_here = pltpu.make_async_copy(late_src, late_at(0, 0, 0), q_own)
-    late_mate = remote(late_src, late_at(1, 0, 0), mate_send, mate_recv, mate)
+    late_mate = remote(x_ref, xm, mate_send, mate_recv, mate)
 
     @pl.when(swapped)
     def _():
         for j in range(CHUNKS):
             x_over(j).start()
-
-    late_here.start()
-    late_mate.start()
 
     @pl.when(swapped)
     def _():
@@ -152,7 +138,7 @@
 
     def ring(s, j):
         place = pl.ds(mine + starts[j], sizes[j])
-        end = ends[0 if j in (0, CHUNKS - 1) else 1]
+        end = up if starts[j] < side else down
         return remote(xb.at[s, place], xb.at[s + 1, place], ring_send.at[s, j], got.at[s + 1, 0, j], end)
 
     def share(s, j):
@@ -269,7 +255,7 @@
             copy.start()
 
     def outer_stage(s):
-        for k, stage_of in enumerate((sum_core, sum_x, sum_y, gather_y, gather_x, gather_core, outer_step)):
+        for k, stage_of in enumerate((sum_core, sum_x, sum_y, gather_y, gather_x, gather_core)):
             pl.when(s == k)(stage_of)
 
     acc[...] = jnp.zeros_like(acc)
@@ -279,6 +265,7 @@
         for j in range(CHUNKS):
             pass_on(s, j, True)
         outer_stage(s)
+        pl.when(s == 2)(late_mate.start)
         return carry
 
     lax.fori_loop(0, half, early, 0)
@@ -300,28 +287,26 @@
         outer_stage(s)
         return carry
 
-    lax.fori_loop(half, nz - 1, late, 0)
-
-    lanes = [(lane, way, half if lane == way else half - 1) for lane in range(2) for way in range(2)]
-
-    def late_send(lane, step, way):
-        return remote(
-            late_at(lane, step - 1, way), late_at(lane, step, way),
-            q_send.at[lane, way, step - 1], q_recv.at[lane, way, step - 1], (up, down)[way],
-        )
-
-    late_here.wait()
+    lax.fori_loop(half, last, late, 0)
+
+    def late_send(lane, way):
+        source = (x_ref, xm)[lane].at[pl.ds(way * side, side)]
+        slot = xq.at[pl.ds((lane * 2 + way) * side, side)]
+        return remote(source, slot, q_send.at[lane, way], q_recv.at[lane, way], (down, up)[way])
+
+    late = [late_send(lane, way) for lane in range(2) for way in range(2)]
+
+    pass_on(last, 0, False)
+    forward(last - 2)
+    backward(last - 2)
+    pass_on(last, 1, False)
+    forward(last - 1)
+    backward(last - 1)
     late_mate.wait()
-    for lane, way, most in lanes:
-        late_send(lane, 1, way).start()
-
-    last = nz - 1
-    pass_on(last, 0, False)
-    forward(last - 1)
-    pass_on(last, 1, False)
-    backward(last - 1)
     pass_on(last, 2, False)
     pass_on(last, 3, False)
+    for copy in late:
+        copy.start()
     forward(last)
 
     def tile_at(t):
@@ -353,12 +338,9 @@
                 pltpu.make_async_copy(ref, ref, relay_recv.at[t // 2]).wait()
                 back_relay(t).start()
 
-    for step in range(1, half + 1):
-        for lane, way, most in lanes:
-            if step <= most:
-                late_send(lane, step, way).wait_recv()
-            if step < most:
-                late_send(lane, step + 1, way).start()
+    outer_step()
+    for copy in late:
+        copy.wait_recv()
 
     outputs = jnp.dot(xq[...], home[...], preferred_element_type=jnp.float32) * inv_root
     target = xq[:, pl.ds(col_home, columns)].astype(jnp.float32)
@@ -400,9 +382,8 @@
         for t in range(1, TILES, 2):
             back_relay(t).wait_send()
 
-    for lane, way, most in lanes:
-        for step in range(1, most + 1):
-            late_send(lane, step, way).wait_send()
+    for copy in late:
+        copy.wait_send()
     for t in range(TILES):
         out_here(t).wait()
     for copy in stores:
@@ -413,14 +394,14 @@
             share(s, j).wait_send()
         return carry
 
-    lax.fori_loop(0, nz, drain, 0)
+    lax.fori_loop(0, last + 1, drain, 0)
 
     def drain_ring(s, carry):
         for j in range(CHUNKS):
             ring(s, j).wait_send()
         return carry
 
-    lax.fori_loop(0, nz - 1, drain_ring, 0)
+    lax.fori_loop(0, last, drain_ring, 0)
 
 
 def window(nz, ny, fragment, tokens, weight, anchor, momentum):
@@ -442,13 +423,14 @@
         in_specs=[pl.BlockSpec(memory_space=pltpu.SMEM), whole, whole, whole, whole],
         out_specs=(result, result, result),
         scratch_shapes=[
-            pltpu.VMEM((nz, 2 * (rows - LATE_ROWS), width), jnp.bfloat16),
-            pltpu.VMEM((2 * nz * LATE_ROWS, width), jnp.bfloat16),
+            pltpu.VMEM((nz - 1, 2 * rows, width), jnp.bfloat16),
+            pltpu.VMEM((2 * rows, width), jnp.bfloat16),
+            pltpu.VMEM((rows, width), jnp.bfloat16),
             pltpu.VMEM((width, columns), jnp.bfloat16),
             pltpu.VMEM((width, columns), jnp.bfloat16),
             pltpu.VMEM((width, columns), jnp.float32),
-            pltpu.VMEM((2 * (rows - LATE_ROWS), columns), jnp.bfloat16),
-            pltpu.VMEM((2 * nz * LATE_ROWS, columns), jnp.bfloat16),
+            pltpu.VMEM((2 * rows, columns), jnp.bfloat16),
+            pltpu.VMEM((2 * rows, columns), jnp.bfloat16),
             pltpu.VMEM((width, columns), jnp.bfloat16),
             pltpu.VMEM((width // 2, columns), jnp.bfloat16),
             pltpu.VMEM((width, columns), jnp.bfloat16),
@@ -461,9 +443,9 @@
             pltpu.VMEM((frag_rows // 4, columns), jnp.float32),
             pltpu.VMEM((ny - 1, frag_rows // (4 * ny), columns), jnp.float32),
             pltpu.VMEM((frag_rows, columns), jnp.float32),
-            dma((CHUNKS,)), dma((W_PIECES,)), dma((W_PIECES,)), dma((nz, 2, CHUNKS)), dma((nz - 1, CHUNKS)),
-            dma((nz, CHUNKS)), dma((TILES,)), dma((TILES // 2,)), dma((TILES // 2,)), dma((TILES,)),
-            dma, dma, dma, dma((2, 2, nz // 2)), dma((2, 2, nz // 2)), dma((TILES,)), dma((3,)), dma((2,)),
+            dma((CHUNKS,)), dma((W_PIECES,)), dma((W_PIECES,)), dma((nz - 1, 2, CHUNKS)), dma((nz - 2, CHUNKS)),
+            dma((nz - 1, CHUNKS)), dma((TILES,)), dma((TILES // 2,)), dma((TILES // 2,)), dma((TILES,)),
+            dma, dma, dma((2, 2)), dma((2, 2)), dma((TILES,)), dma((3,)), dma((2,)),
             dma, dma, dma, dma, dma((ny - 1,)), dma((ny - 1,)), dma((ny - 1,)), dma((ny - 1,)), dma, dma, dma, dma,
         ],
         cost_estimate=pl.CostEstimate(flops=flops, bytes_accessed=8 << 20, transcendentals=0),

time: 119 us -> 123 us (1.034)
  Pallas kernels: 115 us -> 119 us
    pallas_call x1, Pallas kernels: 115 us -> 119 us  [window(): pl.pallas_call(functools.partial(step_kernel, nz, ny, total_rows), out_sh...]
where the time goes in v4:
time: 123 us
  Pallas kernels  119 us (97%)
  local copies, waits for them, and re-layouts  2.91 us (2%)
  between operations  1.29 us (1%)
    pallas_call x1, Pallas kernels, window(): pl.pallas_call(functools.partial(step_kernel, nz, ny, total_rows), out_sh...  119 us
    unnamed x3, local copies, waits for them, and re-layouts  2.91 us

profile of v4, /device:TPU:1, one launch (start us, length us, event | category | flops | bytes accessed | tf_op | source)
XLA Modules:
  0.0 122.9 jit_solution(6036171376553552311)
XLA Ops:
  1.3 118.7 %shard_map.76 = (bf16[4096,256]{1,0:T(8,128)(2,1)S(1)}, f32[512,256]{1,0:T(8,128)S(1)}, f32[512,256]{1,0:T(8,128)S(1)}) custom-call(s32[1]{0:T(128)S(6)} %copy.14.frag_ref, bf16[128,4096]{1,0:T(8,128)(2,1)} %bitcast.5, bf16[4096,256]{1,0:T(8,128)(2,1)} %bitcast.4, f32[512,256]{1,0:T(8,128)} %a_ref.1, f32[512,256]{1,0:T(8,128)} %m_ref.1), custom_call_target="tpu_custom_call" | custom-call | flops 8589934592 | bytes 8388608 | tf_op jit(solution)/shard_map/pallas_call | solution.py:416
  120.0 1.3 %copy.11 = bf16[1,4096,256]{2,1,0:T(8,128)(2,1)} copy(bf16[1,4096,256]{2,1,0:T(8,128)(2,1)S(1)} %bitcast.3) | data formatting | bytes 4194304
  121.3 0.8 copy.12
  122.1 0.8 copy.13

commit v5 on v3

--- a/solution.py
+++ b/solution.py
@@ -310,11 +310,6 @@
             q_send.at[lane, way, step - 1], q_recv.at[lane, way, step - 1], (up, down)[way],
         )
 
-    late_here.wait()
-    late_mate.wait()
-    for lane, way, most in lanes:
-        late_send(lane, 1, way).start()
-
     last = nz - 1
     pass_on(last, 0, False)
     forward(last - 1)
@@ -322,6 +317,10 @@
     backward(last - 1)
     pass_on(last, 2, False)
     pass_on(last, 3, False)
+    late_here.wait()
+    late_mate.wait()
+    for lane, way, most in lanes:
+        late_send(lane, 1, way).start()
     forward(last)
 
     def tile_at(t):

time: 119 us -> 118 us (level)
  Pallas kernels: 115 us -> 113 us
    pallas_call x1, Pallas kernels: 115 us -> 113 us  [window(): pl.pallas_call(functools.partial(step_kernel, nz, ny, total_rows), out_sh...]
where the time goes in v5:
time: 118 us
  Pallas kernels  113 us (96%)
  local copies, waits for them, and re-layouts  2.91 us (2%)
  between operations  1.29 us (1%)
    pallas_call x1, Pallas kernels, window(): pl.pallas_call(functools.partial(step_kernel, nz, ny, total_rows), out_sh...  113 us
    unnamed x3, local copies, waits for them, and re-layouts  2.91 us

profile of v5, /device:TPU:1, one launch (start us, length us, event | category | flops | bytes accessed | tf_op | source)
XLA Modules:
  0.0 117.5 jit_solution(81064339733677667)
XLA Ops:
  1.3 113.4 %shard_map.76 = (bf16[4096,256]{1,0:T(8,128)(2,1)S(1)}, f32[512,256]{1,0:T(8,128)S(1)}, f32[512,256]{1,0:T(8,128)S(1)}) custom-call(s32[1]{0:T(128)S(6)} %copy.14.frag_ref, bf16[128,4096]{1,0:T(8,128)(2,1)} %bitcast.5, bf16[4096,256]{1,0:T(8,128)(2,1)} %bitcast.4, f32[512,256]{1,0:T(8,128)} %a_ref.1, f32[512,256]{1,0:T(8,128)} %m_ref.1), custom_call_target="tpu_custom_call" | custom-call | flops 8589934592 | bytes 8388608 | tf_op jit(solution)/shard_map/pallas_call | solution.py:434
  114.6 1.3 %copy.11 = bf16[1,4096,256]{2,1,0:T(8,128)(2,1)} copy(bf16[1,4096,256]{2,1,0:T(8,128)(2,1)S(1)} %bitcast.3) | data formatting | bytes 4194304
  116.0 0.8 copy.12
  116.8 0.8 copy.13
